TPU v7x, 1024 devices: a whole 4x8x16 slice. The times are simulated.
1024 devices in a mesh: dp: 128 (over z, y_hi, core), mp: 8 (over x, y_lo).
Axes of the slice: x: 4, y: 8 (y_hi: 4, y_lo: 2; y = y_hi * 2 + y_lo), z: 16, core: 2. Of those that a mesh axis runs over, the one named last changes fastest.
Arguments:
- student_in: bfloat16 [128, 6144], P(None, 'mp'), may hold values from -6 to 6
- teacher_hidden: bfloat16 [8192, 128], P('dp'), may hold values from -6 to 6
- w_up: bfloat16 [24576, 6144], P('dp', 'mp'), may hold values from -0.078125 to 0.078125
- w_down: bfloat16 [24576, 6144], P('dp', 'mp'), may hold values from -0.0390625 to 0.0390625
- w_proj: bfloat16 [8192, 6144], P('dp', 'mp'), may hold values from -0.0625 to 0.0625
Outputs:
- grad_up: float32 [24576, 6144], P('dp', 'mp')
- grad_down: float32 [24576, 6144], P('dp', 'mp')
- grad_proj: float32 [8192, 6144], P('dp', 'mp')
All inputs are finite; a program needn't handle non-finite values.
Results may differ from a plain program's by a relative error of at most 0.005.
Values may be sent and summed in bfloat16 or wider, within the bound.
A program may use at most 32 MiB of HBM per device.

v0:
```python
import math

import jax
import jax.numpy as jnp
from jax import lax
from jax.sharding import PartitionSpec as P


def contract_first(left, right):
    return lax.dot_general(
        left, right, (((0,), (0,)), ((), ())), preferred_element_type=jnp.float32
    )


def contract_last(left, right):
    return lax.dot_general(
        left, right, (((1,), (1,)), ((), ())), preferred_element_type=jnp.float32
    )


def body(student_in, teacher_hidden, w_up, w_down, w_proj):
    tokens_all = student_in.shape[0]
    partial_pre = contract_last(w_up, student_in)
    pre = lax.psum(partial_pre, "mp")
    active = jnp.maximum(pre, 0.0)
    hidden = (active * active).astype(jnp.bfloat16)
    student_part = contract_first(hidden, w_down)
    target_part = contract_first(teacher_hidden, w_proj)
    student_out, target = (
        lax.psum_scatter(student_part, "dp", scatter_dimension=0, tiled=True),
        lax.psum_scatter(target_part, "dp", scatter_dimension=0, tiled=True),
    )
    residual = student_out - target
    d_local = (residual * (1.0 / math.sqrt(tokens_all))).astype(jnp.bfloat16)
    piece = lax.all_gather(d_local, "dp", axis=0, tiled=True)
    proj_acc = jnp.zeros(w_proj.shape, jnp.float32)
    down_acc = jnp.dot(hidden, piece, preferred_element_type=jnp.float32)
    proj_acc = proj_acc - jnp.dot(teacher_hidden, piece, preferred_element_type=jnp.float32)
    grad_cols = contract_last(w_down, piece)
    d_hidden = lax.psum(grad_cols, "mp")
    d_pre = (d_hidden * (2.0 * active)).astype(jnp.bfloat16)
    grad_up = jnp.dot(d_pre, student_in, preferred_element_type=jnp.float32)
    return (grad_up, down_acc, proj_acc)


def solution(mesh):
    return jax.shard_map(
        body,
        mesh=mesh,
        in_specs=(P(None, "mp"), P("dp", None), P("dp", "mp"), P("dp", "mp"), P("dp", "mp")),
        out_specs=(P("dp", "mp"), P("dp", "mp"), P("dp", "mp")),
        check_vma=False,
    )
```

profile of v0, /device:TPU:1, one launch (start us, length us, event | category | flops | bytes accessed | tf_op | source)
XLA Modules:
  0.0 1422.6 jit_solution(12933316683525922294)
XLA Ops:
  7.2 0.0 copy-start
  7.2 0.0 all-reduce.7.cloned.1.call-start
  7.2 0.0 copy-start.4
  7.2 1.9 fusion.17
  9.2 0.0 copy-start.3
  9.2 0.0 all-reduce.7.cloned.1.call-update
  9.2 0.0 all-reduce.11.cloned.1.call-start
  9.2 0.0 copy-done.4
  9.3 0.8 copy-done.3
  10.1 1.0 fusion.18
  11.0 97.7 %all-reduce.7.cloned.1.call-done = f32[192,128]{1,0:T(8,128)} async-done(((f32[192,128]{1,0:T(8,128)}), f32[192,128]{1,0:T(8,128)}) %all-reduce.7.cloned.1.call-update) | async-done | bytes 98320 | tf_op jit(solution)/shard_map/psum | solution.py:24
  108.7 0.0 copy-done
  108.7 1.9 fusion.8
  110.6 0.0 all-reduce.11.cloned.1.call-update
  110.6 0.0 all-reduce.9.cloned.1.call-start
  110.7 1.3 dynamic-slice
  112.0 1062.7 %all-reduce.11.cloned.1.call-done = (f32[128,768]{1,0:T(8,128)}, f32[128,768]{1,0:T(8,128)}) async-done(((f32[128,768]{1,0:T(8,128)}, f32[128,768]{1,0:T(8,128)}), (f32[128,768]{1,0:T(8,128)}, f32[128,768]{1,0:T(8,128)})) %all-reduce.11.cloned.1.call-update) | async-done | bytes 786448
  1174.6 1.4 convert_bitcast_fusion
  1176.0 152.8 %all-gather = bf16[128,1,768]{2,1,0:T(2,128)(2,1)S(1)} all-gather(bf16[1,1,768]{2,1,0:T(2,128)(2,1)S(1)} %convert_bitcast_fusion), channel_id=1, replica_groups=mesh['dp'=128,'mp'=8] {'dp'}, dimensions={0}, use_global_device_ids=true | all-gather | bytes 198144 | tf_op jit(solution)/shard_map/all_gather | solution.py:35
  1328.9 0.9 convolution_bitcast_fusion
  1329.7 0.0 copy-start.1
  1329.8 0.0 all-reduce.9.cloned.1.call-update
  1329.8 0.9 copy-done.1
  1330.6 1.0 fusion.2
  1331.7 0.0 copy-start.2
  1331.7 0.8 fusion
  1332.5 81.6 %all-reduce.9.cloned.1.call-done = f32[192,128]{1,0:T(8,128)} async-done(((f32[192,128]{1,0:T(8,128)}), f32[192,128]{1,0:T(8,128)}) %all-reduce.9.cloned.1.call-update) | async-done | bytes 98320 | tf_op jit(solution)/shard_map/psum | solution.py:40
  1414.2 0.0 copy-done.2
  1414.2 1.9 fusion.5
Async XLA Ops:
  7.2 101.6 %copy-start = (bf16[192,768]{1,0:T(8,128)(2,1)S(1)}, bf16[192,768]{1,0:T(8,128)(2,1)}, u32[]{:S(2)}) copy-start(bf16[192,768]{1,0:T(8,128)(2,1)} %param.8) | copy-start | bytes 884740
  7.2 101.5 %all-reduce.7.cloned.1.call-start = ((), (), s32[]{:S(2)}) async-start(), calls=%async_computation | async-start | bytes 196608 | tf_op jit(solution)/shard_map/psum | solution.py:24
  7.2 2.0 copy-start.4
  9.2 0.9 copy-start.3
  9.2 1165.4 %all-reduce.11.cloned.1.call-start = ((), (), s32[]{:S(2)}) async-start(), calls=%async_computation.2 | async-start | bytes 1572864
  110.6 1303.5 %all-reduce.9.cloned.1.call-start = ((), (), s32[]{:S(2)}) async-start(), calls=%async_computation.1 | async-start | bytes 196608 | tf_op jit(solution)/shard_map/psum | solution.py:40
  1329.7 0.9 copy-start.1
  1331.7 82.5 %copy-start.2 = (bf16[128,768]{1,0:T(8,128)(2,1)S(1)}, bf16[128,768]{1,0:T(8,128)(2,1)}, u32[]{:S(2)}) copy-start(bf16[128,768]{1,0:T(8,128)(2,1)} %param.5) | copy-start | bytes 589828
Sparse Core Ops, SparseCore 0:
  12.1 96.5 all-reduce.6
  113.3 1061.2 all-reduce.10
  1329.9 84.2 all-reduce.8
where the time goes:
time: 1430 us; the launch traced here: 1420 us
  waiting for transfers between devices  1240 us (87%)
  blocking collectives  153 us (11%)
    unnamed x4, waiting for transfers between devices  1060 us
    all_gather x1, blocking collectives, body(): piece = lax.all_gather(d_local, 'dp', axis=0, tiled=True)  153 us
    psum x1, waiting for transfers between devices, body(): pre = lax.psum(partial_pre, 'mp')  97.7 us
    psum x1, waiting for transfers between devices, body(): d_hidden = lax.psum(grad_cols, 'mp')  81.6 us
  transfers between devices with their start and end apart: 3, of which 3 were waited for; matrix products, arithmetic and copies ran while one was open for 0% of the time, Pallas kernels for 0%

commit v1 on v0

v1 whole, which is shorter than its diff:
```python
import math

import jax
import jax.numpy as jnp
from jax import lax
from jax.experimental import pallas as pl
from jax.experimental.pallas import tpu as pltpu
from jax.sharding import PartitionSpec as P

F32, BF16 = jnp.float32, jnp.bfloat16
NZ, NY, NC, NX, NL = 16, 4, 2, 4, 2
NM = NX * NL
MESH = pl.DeviceIdType.MESH

WINDOW = [(dz, dy) for dz in (-2, 1, -1, 0) for dy in (2, 1, 3, 0) if dz or dy]
STRIDES = (6, -6, 2, -2)


def nt(a, b):
    return lax.dot_general(a, b, (((1,), (1,)), ((), ())), preferred_element_type=F32)


def tn(a, b):
    return lax.dot_general(a, b, (((0,), (0,)), ((), ())), preferred_element_type=F32)


def nn(a, b):
    return jnp.dot(a, b, preferred_element_type=F32)


def step_kernel(
    x_h, th_h, wu_h, wd_h, wp_h,
    gu_h, gd_h, gp_h,
    x, th, wu, wd, wp, gu, gd, gp,
    pre_s, pre_r, act, hid, ht, ht2, tgt, tgt_r,
    res_s, res_r, win, far_r, piece, dfull, dh_s, dh_r, dpt,
    in_sem, out_sem, core_ss, core_rs,
    a1_ss, a1_rs, a2_ss, a2_rs, b1_ss, b1_rs, b2_ss, b2_rs, c_ss, c_rs, d1_ss, d1_rs, d2_ss, d2_rs,
):
    ff = wu.shape[0]
    half = x.shape[0] // 2
    cols = piece.shape[1]
    dp, mp = lax.axis_index("dp"), lax.axis_index("mp")
    z, y, c = dp // (NY * NC), (dp // NC) % NY, dp % NC
    oc = 1 - c
    own_half = mp // (NM // 2)
    tok = mp % (NM // 2)

    def at(dz, dy):
        return lax.rem(z + dz + NZ, NZ), lax.rem(y + dy + NY, NY)

    def device(zz, yy, cc, mm):
        return (zz * (NY * NC) + yy * NC + cc, mm)

    barrier = pltpu.get_barrier_semaphore()
    senders = [(-s, 0) for s in STRIDES if (s, 0) not in WINDOW] + [(-dz, -dy) for dz, dy in WINDOW]
    for dz, dy in senders:
        zz, yy = at(dz, dy)
        pl.semaphore_signal(barrier, inc=1, device_id=device(zz, yy, c, mp), device_id_type=MESH)
    for dc in range(NC):
        for dm in range(NM):
            if dc or dm:
                cc, mm = lax.rem(c + dc, NC), lax.rem(mp + dm, NM)
                pl.semaphore_signal(barrier, inc=1, device_id=device(z, y, cc, mm), device_id_type=MESH)

    loads = [
        pltpu.make_async_copy(src, dst, in_sem.at[i])
        for i, (src, dst) in enumerate(((x_h, x), (wu_h, wu), (th_h, th), (wp_h, wp), (wd_h, wd.at[c])))
    ]
    for load in loads:
        load.start()
    sent = []

    def send(src, dst, ss, rs, dev):
        copy = pltpu.make_async_remote_copy(
            src_ref=src, dst_ref=dst, send_sem=ss, recv_sem=rs, device_id=dev, device_id_type=MESH
        )
        copy.start()
        sent.append(copy)

    def arrived(dst, sem):
        pltpu.make_async_copy(dst, dst, sem).wait()

    loads[0].wait()
    loads[1].wait()
    part = nt(x[...], wu[...])
    for m in range(NM):
        pre_s[m, :, :ff] = part[16 * m : 16 * m + 16]
    pl.semaphore_wait(barrier, len(senders) + NC * NM - 1)
    for d in range(1, NM):
        mm = lax.rem(mp + d, NM)
        send(pre_s.at[mm], pre_r.at[mp], a1_ss.at[d], a1_rs.at[mp], device(z, y, c, mm))
    partner = device(z, y, oc, mp)
    send(wd_h, wd.at[c], core_ss.at[0], core_rs.at[0], partner)

    loads[2].wait()
    loads[3].wait()
    goal = tn(th[...], wp[...])
    for i in range(NC):
        tgt[i] = goal[half * i : half * i + half]
    send(tgt.at[oc], tgt_r, core_ss.at[1], core_rs.at[1], partner)

    total = pre_s[mp]
    for d in range(1, NM):
        mm = lax.rem(mp + d, NM)
        arrived(pre_r.at[mm], a1_rs.at[mm])
        total = total + pre_r[mm]
    active = jnp.maximum(total, 0.0)
    hid[...] = (active * active).astype(BF16)
    for d in range(1, NM):
        mm = lax.rem(mp + d, NM)
        send(hid, ht.at[c, tok], a2_ss.at[d], a2_rs.at[c * (NM // 2) + tok], device(z, y, own_half, mm))
    keep = pltpu.make_async_copy(hid, ht.at[c, tok], a2_rs.at[c * (NM // 2) + tok])
    give = pltpu.make_async_remote_copy(
        src_ref=hid, dst_ref=ht.at[c, tok], send_sem=a2_ss.at[0], recv_sem=a2_rs.at[c * (NM // 2) + tok],
        device_id=partner, device_id_type=MESH,
    )

    @pl.when(own_half == c)
    def _():
        keep.start()

    @pl.when(own_half != c)
    def _():
        give.start()

    act[...] = 2.0 * active
    loads[4].wait()
    arrived(wd.at[oc], core_rs.at[0])
    arrived(tgt_r, core_rs.at[1])
    base = tgt[c] + tgt_r[...]
    for i in range(NC):
        for t in range(NM // 2):
            arrived(ht.at[i, t], a2_rs.at[i * (NM // 2) + t])

    part = -base
    for i in range(NC):
        part = part + nn(ht[i].reshape(half, ht.shape[-1])[:, :ff], wd[i])
    groups = half // 8
    for h in range(2):
        res_s[groups * h : groups * h + groups] = part[:, cols * h : cols * h + cols].reshape(groups, 8, cols)
    for j, (dz, dy) in enumerate(WINDOW):
        zz, yy = at(dz, dy)
        send(res_s.at[yy * 4 + lax.rem(zz, 4)], res_r.at[j], b1_ss.at[j], b1_rs.at[j], device(zz, yy, c, mp))
    send(ht.at[oc], ht2, core_ss.at[2], core_rs.at[2], partner)
    total = res_s[y * 4 + lax.rem(z, 4)]
    for j in reversed(range(len(WINDOW))):
        arrived(res_r.at[j], b1_rs.at[j])
        total = total + res_r[j]
    win[...] = total
    for j, s in enumerate(STRIDES):
        zz, yy = at(s, 0)
        send(win, far_r.at[j], b2_ss.at[j], b2_rs.at[j], device(zz, yy, c, mp))
    for j in range(len(STRIDES)):
        arrived(far_r.at[j], b2_rs.at[j])
    residual = (far_r[0] + far_r[1]) + (far_r[2] + far_r[3])
    piece[...] = (residual * (1.0 / math.sqrt(2 * half))).astype(BF16)
    mine = y * 4 + lax.rem(z + 2, 4)
    for j, (dz, dy) in enumerate(WINDOW):
        zz, yy = at(dz, dy)
        send(piece, dfull.at[c, mine], c_ss.at[j], c_rs.at[j], device(zz, yy, c, mp))
    dfull[c, mine] = piece[...]
    for j, (dz, dy) in enumerate(WINDOW):
        zz, yy = at(-dz, -dy)
        arrived(dfull.at[c, yy * 4 + lax.rem(zz + 2, 4)], c_rs.at[j])
    send(dfull.at[c], dfull.at[c], core_ss.at[3], core_rs.at[3], partner)

    def d_half(i, h):
        return dfull[i, groups * h : groups * h + groups].reshape(half, cols)

    d_own = [d_half(c, h) for h in range(2)]
    for i in range(NC):
        part = nt(d_own[0], wd[i, :, :cols]) + nt(d_own[1], wd[i, :, cols:])
        dh_s[i, :, :, :ff] = part.reshape(NM // 2, 16, ff)
    for e in range(NC):
        for d in range(NM // 2):
            if e or d:
                i, t = lax.rem(c + e, NC), lax.rem(tok + d, NM // 2)
                k = e * (NM // 2) + d
                send(dh_s.at[i, t], dh_r.at[mp], d1_ss.at[k], d1_rs.at[mp], device(z, y, i, c * (NM // 2) + t))
    keep2 = pltpu.make_async_copy(dh_s.at[c, tok], dh_r.at[mp], d1_rs.at[mp])
    give2 = pltpu.make_async_remote_copy(
        src_ref=dh_s.at[c, tok], dst_ref=dh_r.at[mp], send_sem=d1_ss.at[0], recv_sem=d1_rs.at[mp],
        device_id=device(z, y, c, c * (NM // 2) + tok), device_id_type=MESH,
    )

    @pl.when(own_half == c)
    def _():
        keep2.start()

    @pl.when(own_half != c)
    def _():
        give2.start()

    arrived(dfull.at[oc], core_rs.at[3])
    arrived(ht2, core_rs.at[2])
    d_other = [d_half(oc, h) for h in range(2)]
    h_own = ht[c].reshape(half, ht.shape[-1])[:, :ff]
    h_other = ht2[...].reshape(half, ht.shape[-1])[:, :ff]
    d_nat = [[d_half(i, h) for h in range(2)] for i in range(NC)]
    for h in range(2):
        gd[:, cols * h : cols * h + cols] = tn(h_own, d_own[h]) + tn(h_other, d_other[h])
        gp[:, cols * h : cols * h + cols] = -(nn(th[:, :half], d_nat[0][h]) + nn(th[:, half:], d_nat[1][h]))
    outs = [
        pltpu.make_async_copy(src, dst, out_sem.at[i])
        for i, (src, dst) in enumerate(((gd, gd_h), (gp, gp_h), (gu, gu_h)))
    ]
    outs[0].start()
    outs[1].start()

    for m in range(NM):
        arrived(dh_r.at[m], d1_rs.at[m])
    total = dh_r[0]
    for m in range(1, NM):
        total = total + dh_r[m]
    dpt[mp] = (total * act[...]).astype(BF16)
    for d in range(1, NM):
        mm = lax.rem(mp + d, NM)
        send(dpt.at[mp], dpt.at[mp], d2_ss.at[d], d2_rs.at[mp], device(z, y, c, mm))
    for d in range(1, NM):
        mm = lax.rem(mp + d, NM)
        arrived(dpt.at[mm], d2_rs.at[mm])
    gu[...] = tn(dpt[...].reshape(2 * half, dpt.shape[-1])[:, :ff], x[...])
    outs[2].start()
    for copy in sent:
        copy.wait_send()

    @pl.when(own_half != c)
    def _():
        give.wait_send()
        give2.wait_send()

    for out in outs:
        out.wait()


def body(student_in, teacher_hidden, w_up, w_down, w_proj):
    tokens, width = student_in.shape
    ff, td = w_up.shape[0], w_proj.shape[0]
    half, cols = tokens // 2, width // 2
    wide = 256
    any_ = pl.BlockSpec(memory_space=pl.ANY)
    sem = pltpu.SemaphoreType.DMA
    vm = pltpu.VMEM
    scratch = [
        vm((tokens, width), BF16), vm((td, tokens), BF16), vm((ff, width), BF16), vm((NC, ff, width), BF16),
        vm((td, width), BF16), vm((ff, width), F32), vm((ff, width), F32), vm((td, width), F32),
        vm((NM, 16, wide), F32), vm((NM, 16, wide), F32), vm((16, wide), F32), vm((16, wide), BF16),
        vm((NC, NM // 2, 16, wide), BF16), vm((NM // 2, 16, wide), BF16),
        vm((NC, half, width), F32), vm((half, width), F32),
        vm((16, 8, cols), F32), vm((15, 8, cols), F32), vm((8, cols), F32), vm((4, 8, cols), F32),
        vm((8, cols), BF16), vm((NC, 16, 8, cols), BF16),
        vm((NC, NM // 2, 16, wide), F32), vm((NM, 16, wide), F32), vm((NM, 16, wide), BF16),
        sem((5,)), sem((3,)), sem((4,)), sem((4,)),
        sem((8,)), sem((8,)), sem((8,)), sem((8,)), sem((15,)), sem((15,)), sem((4,)), sem((4,)),
        sem((15,)), sem((15,)), sem((8,)), sem((8,)), sem((8,)), sem((8,)),
    ]
    return pl.pallas_call(
        step_kernel,
        out_shape=(
            jax.ShapeDtypeStruct((ff, width), F32),
            jax.ShapeDtypeStruct((ff, width), F32),
            jax.ShapeDtypeStruct((td, width), F32),
        ),
        in_specs=[any_] * 5,
        out_specs=(any_,) * 3,
        scratch_shapes=scratch,
        compiler_params=pltpu.CompilerParams(
            collective_id=0, has_side_effects=True, vmem_limit_bytes=40 * 1024 * 1024
        ),
        name="distill_step",
    )(student_in, teacher_hidden, w_up, w_down, w_proj)


def solution(mesh):
    return jax.shard_map(
        body,
        mesh=mesh,
        in_specs=(P(None, "mp"), P("dp", None), P("dp", "mp"), P("dp", "mp"), P("dp", "mp")),
        out_specs=(P("dp", "mp"), P("dp", "mp"), P("dp", "mp")),
        check_vma=False,
    )
```

time: 1430 us -> 67.4 us (0.05)
  waiting for transfers between devices: 1240 us -> 0 us
  blocking collectives: 153 us -> 0 us
  Pallas kernels: 0 us -> 59.7 us
    unnamed x4 -> x0, waiting for transfers between devices: 1060 us -> none
    psum x2 -> x0, waiting for transfers between devices: 179 us -> none  [the longest x1 97.7 us: body(): pre = lax.psum(partial_pre, 'mp')]
    all_gather x1 -> x0, blocking collectives: 153 us -> none  [body(): piece = lax.all_gather(d_local, 'dp', axis=0, tiled=True)]
    pallas_call x0 -> x1, Pallas kernels: none -> 59.7 us  [body(): pl.pallas_call(step_kernel, out_shape=(jax.ShapeDtypeStruct((ff, width),...]
  transfers between devices with their start and end apart: 3 -> 0, of which waited for: 3 -> 0; matrix products, arithmetic and copies ran while one was open for 0% -> 0% of each run, Pallas kernels for 0% -> 0%
where the time goes in v1:
time: 67.4 us; the launch traced here: 67.1 us
  Pallas kernels  59.7 us (89%)
  local copies, waits for them, and re-layouts  6.76 us (10%)
    pallas_call x1, Pallas kernels, body(): pl.pallas_call(step_kernel, out_shape=(jax.ShapeDtypeStruct((ff, width),...  59.7 us
    unnamed x13, local copies, waits for them, and re-layouts  6.76 us

profile of v1, /device:TPU:1, one launch (start us, length us, event | category | flops | bytes accessed | tf_op | source)
XLA Modules:
  0.0 67.1 jit_solution(7887673547114165933)
XLA Ops:
  0.6 0.0 copy-start
  0.6 1.0 %copy-done = bf16[192,768]{1,0:T(8,128)(2,1)S(1)} copy-done((bf16[192,768]{1,0:T(8,128)(2,1)S(1)}, bf16[192,768]{1,0:T(8,128)(2,1)}, u32[]{:S(2)}) %copy-start) | copy-done | bytes 294936
  1.6 0.0 copy-start.1
  1.6 1.0 %copy-done.1 = bf16[192,768]{1,0:T(8,128)(2,1)S(1)} copy-done((bf16[192,768]{1,0:T(8,128)(2,1)S(1)}, bf16[192,768]{1,0:T(8,128)(2,1)}, u32[]{:S(2)}) %copy-start.1) | copy-done | bytes 294936
  2.6 0.0 copy-start.2
  2.6 0.9 %copy-done.2 = bf16[128,768]{1,0:T(8,128)(2,1)S(1)} copy-done((bf16[128,768]{1,0:T(8,128)(2,1)S(1)}, bf16[128,768]{1,0:T(8,128)(2,1)}, u32[]{:S(2)}) %copy-start.2) | copy-done | bytes 196632
  3.5 0.0 copy-start.3
  3.5 0.9 %copy-done.3 = bf16[64,768]{1,0:T(8,128)(2,1)S(1)} copy-done((bf16[64,768]{1,0:T(8,128)(2,1)S(1)}, bf16[64,768]{1,0:T(8,128)(2,1)}, u32[]{:S(2)}) %copy-start.3) | copy-done | bytes 98328
  4.4 0.0 copy-start.4
  4.4 0.7 %copy-done.4 = bf16[64,128]{1,0:T(8,128)(2,1)S(1)} copy-done((bf16[64,128]{1,0:T(8,128)(2,1)S(1)}, bf16[64,128]{1,0:T(8,128)(2,1)}, u32[]{:S(2)}) %copy-start.4) | copy-done | bytes 16408
  5.1 59.7 %distill_step.1 = (f32[192,768]{1,0:T(8,128)S(1)}, f32[192,768]{1,0:T(8,128)S(1)}, f32[64,768]{1,0:T(8,128)S(1)}) custom-call(bf16[128,768]{1,0:T(8,128)(2,1)S(1)} %copy-done.2, bf16[64,128]{1,0:T(8,128)(2,1)S(1)} %copy-done.4, bf16[192,768]{1,0:T(8,128)(2,1)S(1)} %copy-done, bf16[192,768]{1,0:T(8,128)(2,1)S(1)} %copy-done.1, bf16[64,768]{1,0:T(8,128)(2,1)S(1)} %copy-done.3), custom_call_target="tpu_custom_call" | custom-call | tf_op jit(solution)/shard_map/distill_step/pallas_call | solution.py:258
  64.8 0.8 %copy.11 = f32[192,768]{1,0:T(8,128)} copy(f32[192,768]{1,0:T(8,128)S(1)} %get-tuple-element.6) | data formatting | bytes 1179648
  65.6 0.8 %copy.12 = f32[192,768]{1,0:T(8,128)} copy(f32[192,768]{1,0:T(8,128)S(1)} %get-tuple-element.7) | data formatting | bytes 1179648
  66.4 0.7 %copy.13 = f32[64,768]{1,0:T(8,128)} copy(f32[64,768]{1,0:T(8,128)S(1)} %get-tuple-element.8) | data formatting | bytes 393216
Async XLA Ops:
  0.6 1.0 %copy-start = (bf16[192,768]{1,0:T(8,128)(2,1)S(1)}, bf16[192,768]{1,0:T(8,128)(2,1)}, u32[]{:S(2)}) copy-start(bf16[192,768]{1,0:T(8,128)(2,1)} %wu_h.1) | copy-start | bytes 884740
  1.6 1.0 %copy-start.1 = (bf16[192,768]{1,0:T(8,128)(2,1)S(1)}, bf16[192,768]{1,0:T(8,128)(2,1)}, u32[]{:S(2)}) copy-start(bf16[192,768]{1,0:T(8,128)(2,1)} %wd_h.1) | copy-start | bytes 884740
  2.6 0.9 %copy-start.2 = (bf16[128,768]{1,0:T(8,128)(2,1)S(1)}, bf16[128,768]{1,0:T(8,128)(2,1)}, u32[]{:S(2)}) copy-start(bf16[128,768]{1,0:T(8,128)(2,1)} %x_h.1) | copy-start | bytes 589828
  3.5 0.9 %copy-start.3 = (bf16[64,768]{1,0:T(8,128)(2,1)S(1)}, bf16[64,768]{1,0:T(8,128)(2,1)}, u32[]{:S(2)}) copy-start(bf16[64,768]{1,0:T(8,128)(2,1)} %wp_h.1) | copy-start | bytes 294916
  4.4 0.7 %copy-start.4 = (bf16[64,128]{1,0:T(8,128)(2,1)S(1)}, bf16[64,128]{1,0:T(8,128)(2,1)}, u32[]{:S(2)}) copy-start(bf16[64,128]{1,0:T(8,128)(2,1)} %th_h.1) | copy-start | bytes 49156

commit v2 on v1

v2 whole, which is shorter than its diff:
```python
import math

import jax
import jax.numpy as jnp
from jax import lax
from jax.experimental import pallas as pl
from jax.experimental.pallas import tpu as pltpu
from jax.sharding import PartitionSpec as P

F32, BF16 = jnp.float32, jnp.bfloat16
NZ, NY, NC, NX, NL = 16, 4, 2, 4, 2
NM = NX * NL
MESH = pl.DeviceIdType.MESH

WINDOW = (
    (0, 2), (2, 1), (2, -1), (3, 0), (-3, 0), (1, 1), (1, -1), (-1, 1), (-1, -1),
    (2, 0), (-2, 0), (0, 1), (0, -1), (1, 0), (-1, 0),
)
FAR = ((8, 0), (4, 2), (-4, 2))
MP_ORDER = (5, 3, 4, 2, 6, 7, 1)


def nt(a, b):
    return lax.dot_general(a, b, (((1,), (1,)), ((), ())), preferred_element_type=F32)


def tn(a, b):
    return lax.dot_general(a, b, (((0,), (0,)), ((), ())), preferred_element_type=F32)


def nn(a, b):
    return jnp.dot(a, b, preferred_element_type=F32)


def step_kernel(
    x_h, th_h, wu_h, wd_h, wp_h,
    x, dpt, gd, gp,
    th, wu, wd, wp,
    pre_s, pre_r, act, hid, ht, ht2, tgt, tgt_r,
    res_s, res_r, win, far_r, piece, dfull, dh_s, dh_r,
    go, in_sem, core_ss, core_rs,
    a1_ss, a1_rs, a2_ss, a2_rs, b1_ss, b1_rs, b2_ss, b2_rs, c_ss, c_rs, d1_ss, d1_rs, d2_ss, d2_rs,
):
    ff = wu.shape[0]
    half = x.shape[0] // 2
    cols = piece.shape[1]
    quarter = NM // 2
    dp, mp = lax.axis_index("dp"), lax.axis_index("mp")
    z, y, c = dp // (NY * NC), (dp // NC) % NY, dp % NC
    oc = 1 - c
    mirror = 1 - 2 * c
    own_half = mp // quarter
    tok = mp % quarter

    loads = [
        pltpu.make_async_copy(src, dst, in_sem.at[i])
        for i, (src, dst) in enumerate(((x_h, x), (wu_h, wu), (th_h, th), (wp_h, wp), (wd_h, wd.at[c])))
    ]
    loads[0].start()
    loads[1].start()

    def at(dz, dy, sign=1):
        return lax.rem(z + sign * mirror * dz + NZ, NZ), lax.rem(y + sign * dy + NY, NY)

    def device(zz, yy, cc, mm):
        return (zz * (NY * NC) + yy * NC + cc, mm)

    def owned(zz, yy):
        return lax.rem(yy + 2 * (zz // 4), NY) * 4 + lax.rem(zz, 4)

    def signal(sem, dev):
        pl.semaphore_signal(sem, inc=1, device_id=dev, device_id_type=MESH)

    partner = device(z, y, oc, mp)
    barrier = pltpu.get_barrier_semaphore()
    for d in MP_ORDER:
        signal(barrier, device(z, y, 0, lax.rem(mp + d, NM)))

    @pl.when(c == 1)
    def _():
        signal(barrier, partner)

    for dz, dy in FAR + WINDOW:
        zz, yy = at(dz, dy, -1)
        signal(barrier, device(zz, yy, 1, mp))
    for load in loads[2:]:
        load.start()

    def send(src, dst, ss, rs, dev):
        copy = pltpu.make_async_remote_copy(
            src_ref=src, dst_ref=dst, send_sem=ss, recv_sem=rs, device_id=dev, device_id_type=MESH
        )
        copy.start()
        return copy

    def arrived(dst, sem):
        pltpu.make_async_copy(dst, dst, sem).wait()

    def left(copies):
        for copy in copies:
            copy.wait_send()

    loads[0].wait()
    loads[1].wait()
    part = nt(x[...], wu[...])
    for m in range(NM):
        pre_s[m, :, :ff] = part[16 * m : 16 * m + 16]

    @pl.when(c == 0)
    def _():
        pl.semaphore_wait(barrier, NC * NM - 1)
        signal(go, partner)

    @pl.when(c == 1)
    def _():
        pl.semaphore_wait(go, 1)

    sent = []
    for d in MP_ORDER:
        mm = lax.rem(mp + d, NM)
        sent.append(send(pre_s.at[mm], pre_r.at[mp], a1_ss.at[d], a1_rs.at[mp], device(z, y, c, mm)))
    loads[4].wait()
    sent.append(send(wd.at[c], wd.at[c], core_ss.at[0], core_rs.at[0], partner))

    loads[2].wait()
    loads[3].wait()
    goal = tn(th[...], wp[...])
    for i in range(NC):
        tgt[i] = goal[half * i : half * i + half]
    sent.append(send(tgt.at[oc], tgt_r, core_ss.at[1], core_rs.at[1], partner))

    total = pre_s[mp]
    for d in reversed(MP_ORDER):
        mm = lax.rem(mp + d, NM)
        arrived(pre_r.at[mm], a1_rs.at[mm])
        total = total + pre_r[mm]
    active = jnp.maximum(total, 0.0)
    hid[...] = (active * active).astype(BF16)
    slot = c * quarter + tok
    for d in MP_ORDER:
        mm = lax.rem(mp + d, NM)
        sent.append(send(hid, ht.at[c, tok], a2_ss.at[d], a2_rs.at[slot], device(z, y, own_half, mm)))
    keep = pltpu.make_async_copy(hid, ht.at[c, tok], a2_rs.at[slot])
    give = pltpu.make_async_remote_copy(
        src_ref=hid, dst_ref=ht.at[c, tok], send_sem=a2_ss.at[0], recv_sem=a2_rs.at[slot],
        device_id=partner, device_id_type=MESH,
    )

    @pl.when(own_half == c)
    def _():
        keep.start()

    @pl.when(own_half != c)
    def _():
        give.start()

    act[...] = 2.0 * active

    @pl.when(c == 1)
    def _():
        pl.semaphore_wait(barrier, NC * (len(FAR) + len(WINDOW)))
        signal(go, partner)

    @pl.when(c == 0)
    def _():
        pl.semaphore_wait(go, 1)

    arrived(wd.at[oc], core_rs.at[0])
    arrived(tgt_r, core_rs.at[1])
    base = tgt[c] + tgt_r[...]
    for i in range(NC):
        for t in range(quarter):
            arrived(ht.at[i, t], a2_rs.at[i * quarter + t])

    part = -base
    for i in range(NC):
        part = part + nn(ht[i].reshape(half, ht.shape[-1])[:, :ff], wd[i])
    groups = half // 8
    for h in range(2):
        res_s[groups * h : groups * h + groups] = part[:, cols * h : cols * h + cols].reshape(groups, 8, cols)
    sent_b = []
    for j, (dz, dy) in enumerate(WINDOW):
        zz, yy = at(dz, dy)
        sent_b.append(send(res_s.at[owned(zz, yy)], res_r.at[j], b1_ss.at[j], b1_rs.at[j], device(zz, yy, c, mp)))
    sent.append(send(ht.at[oc], ht2, core_ss.at[2], core_rs.at[2], partner))
    left(sent)

    @pl.when(own_half != c)
    def _():
        give.wait_send()

    mine = owned(z, y)
    total = res_s[mine]
    for j in reversed(range(len(WINDOW))):
        arrived(res_r.at[j], b1_rs.at[j])
        total = total + res_r[j]
    win[...] = total
    for j, (dz, dy) in enumerate(FAR):
        zz, yy = at(dz, dy)
        sent_b.append(send(win, far_r.at[j], b2_ss.at[j], b2_rs.at[j], device(zz, yy, c, mp)))
    left(sent_b[: len(WINDOW)])
    residual = total
    for j in range(len(FAR)):
        arrived(far_r.at[j], b2_rs.at[j])
        residual = residual + far_r[j]
    piece[...] = (residual * (1.0 / math.sqrt(2 * half))).astype(BF16)
    sent = []
    for j, (dz, dy) in enumerate(WINDOW):
        zz, yy = at(dz, dy)
        sent.append(send(piece, dfull.at[c, mine], c_ss.at[j], c_rs.at[j], device(zz, yy, c, mp)))
    dfull[c, mine] = piece[...]
    left(sent_b[len(WINDOW) :])
    for j, (dz, dy) in enumerate(WINDOW):
        zz, yy = at(dz, dy, -1)
        arrived(dfull.at[c, owned(zz, yy)], c_rs.at[j])

    def d_half(i, h):
        return dfull[i, groups * h : groups * h + groups].reshape(half, cols)

    d_own = [d_half(c, h) for h in range(2)]
    sent_d = []
    for e in (1, 0):
        i = lax.rem(c + e, NC)
        part = nt(d_own[0], wd[i, :, :cols]) + nt(d_own[1], wd[i, :, cols:])
        dh_s[i, :, :, :ff] = part.reshape(quarter, 16, ff)
        for d in (2, 1, 3, 0):
            if e or d:
                t = lax.rem(tok + d, quarter)
                dev = device(z, y, i, c * quarter + t)
                sent_d.append(send(dh_s.at[i, t], dh_r.at[mp], d1_ss.at[e * quarter + d], d1_rs.at[mp], dev))
    keep2 = pltpu.make_async_copy(dh_s.at[c, tok], dh_r.at[mp], d1_rs.at[mp])
    give2 = pltpu.make_async_remote_copy(
        src_ref=dh_s.at[c, tok], dst_ref=dh_r.at[mp], send_sem=d1_ss.at[0], recv_sem=d1_rs.at[mp],
        device_id=device(z, y, c, c * quarter + tok), device_id_type=MESH,
    )

    @pl.when(own_half == c)
    def _():
        keep2.start()

    @pl.when(own_half != c)
    def _():
        give2.start()

    sent.append(send(dfull.at[c], dfull.at[c], core_ss.at[3], core_rs.at[3], partner))
    left(sent)
    total = None
    for m in range(NM):
        arrived(dh_r.at[m], d1_rs.at[m])
        total = dh_r[m] if total is None else total + dh_r[m]
    dpt[mp] = (total * act[...]).astype(BF16)
    sent = []
    for d in MP_ORDER:
        mm = lax.rem(mp + d, NM)
        sent.append(send(dpt.at[mp], dpt.at[mp], d2_ss.at[d], d2_rs.at[mp], device(z, y, c, mm)))

    left(sent_d)

    @pl.when(own_half != c)
    def _():
        give2.wait_send()

    arrived(dfull.at[oc], core_rs.at[3])
    arrived(ht2, core_rs.at[2])
    h_own = ht[c].reshape(half, ht.shape[-1])[:, :ff]
    h_other = ht2[...].reshape(half, ht.shape[-1])[:, :ff]
    for h in range(2):
        d_nat = [d_half(i, h) for i in range(NC)]
        gd[:, cols * h : cols * h + cols] = tn(h_own, d_half(c, h)) + tn(h_other, d_half(oc, h))
        gp[:, cols * h : cols * h + cols] = -(nn(th[:, :half], d_nat[0]) + nn(th[:, half:], d_nat[1]))

    for d in MP_ORDER:
        mm = lax.rem(mp + d, NM)
        arrived(dpt.at[mm], d2_rs.at[mm])
    left(sent)


def last_kernel(dpt, x, gd, gp, gu_h, gd_h, gp_h, gu, sem):
    ff = gu.shape[0]
    done = [pltpu.make_async_copy(gd, gd_h, sem.at[0]), pltpu.make_async_copy(gp, gp_h, sem.at[1])]
    for copy in done:
        copy.start()
    rows = dpt[...].reshape(x.shape[0], dpt.shape[-1])[:, :ff]
    step = x.shape[1] // 3
    for i in range(3):
        gu[:, step * i : step * i + step] = tn(rows, x[:, step * i : step * i + step])
        copy = pltpu.make_async_copy(
            gu.at[:, pl.ds(step * i, step)], gu_h.at[:, pl.ds(step * i, step)], sem.at[2 + i]
        )
        copy.start()
        done.append(copy)
    for copy in done:
        copy.wait()


def body(student_in, teacher_hidden, w_up, w_down, w_proj):
    tokens, width = student_in.shape
    ff, td = w_up.shape[0], w_proj.shape[0]
    half, cols = tokens // 2, width // 2
    wide = 256
    hbm, vmem = pl.BlockSpec(memory_space=pltpu.HBM), pl.BlockSpec(memory_space=pltpu.VMEM)
    any_ = pl.BlockSpec(memory_space=pl.ANY)
    sem = pltpu.SemaphoreType.DMA
    vm = pltpu.VMEM
    scratch = [
        vm((td, tokens), BF16), vm((ff, width), BF16), vm((NC, ff, width), BF16),
        vm((td, width), BF16),
        vm((NM, 16, wide), F32), vm((NM, 16, wide), F32), vm((16, wide), F32), vm((16, wide), BF16),
        vm((NC, NM // 2, 16, wide), BF16), vm((NM // 2, 16, wide), BF16),
        vm((NC, half, width), F32), vm((half, width), F32),
        vm((16, 8, cols), F32), vm((15, 8, cols), F32), vm((8, cols), F32), vm((3, 8, cols), F32),
        vm((8, cols), BF16), vm((NC, 16, 8, cols), BF16),
        vm((NC, NM // 2, 16, wide), F32), vm((NM, 16, wide), F32),
        pltpu.SemaphoreType.REGULAR, sem((5,)), sem((4,)), sem((4,)),
        sem((8,)), sem((8,)), sem((8,)), sem((8,)), sem((15,)), sem((15,)), sem((3,)), sem((3,)),
        sem((15,)), sem((15,)), sem((8,)), sem((8,)), sem((8,)), sem((8,)),
    ]
    grads = [jax.ShapeDtypeStruct((rows, width), F32) for rows in (ff, ff, td)]
    x, dpt, gd, gp = pl.pallas_call(
        step_kernel,
        out_shape=(
            jax.ShapeDtypeStruct((tokens, width), BF16),
            jax.ShapeDtypeStruct((NM, 16, wide), BF16),
            *grads[1:],
        ),
        in_specs=[hbm] * 5,
        out_specs=(vmem,) * 4,
        scratch_shapes=scratch,
        compiler_params=pltpu.CompilerParams(
            collective_id=0, has_side_effects=True, vmem_limit_bytes=40 * 1024 * 1024
        ),
        name="distill_step",
    )(*(pltpu.with_memory_space_constraint(a, pltpu.HBM) for a in (student_in, teacher_hidden, w_up, w_down, w_proj)))
    return pl.pallas_call(
        last_kernel,
        out_shape=tuple(grads),
        in_specs=[vmem, vmem, any_, any_],
        out_specs=(any_,) * 3,
        scratch_shapes=[vm((ff, width), F32), sem((5,))],
        compiler_params=pltpu.CompilerParams(vmem_limit_bytes=4 * 1024 * 1024),
        name="grad_up",
    )(dpt, x, gd, gp)


def solution(mesh):
    return jax.shard_map(
        body,
        mesh=mesh,
        in_specs=(P(None, "mp"), P("dp", None), P("dp", "mp"), P("dp", "mp"), P("dp", "mp")),
        out_specs=(P("dp", "mp"), P("dp", "mp"), P("dp", "mp")),
        check_vma=False,
    )
```

time: 67.4 us -> 58.8 us (0.87)
  local copies, waits for them, and re-layouts: 6.76 us -> 0 us
  Pallas kernels: 59.7 us -> 57.8 us
    unnamed x13 -> x0, local copies, waits for them, and re-layouts: 6.76 us -> none
    pallas_call x1 -> x2, Pallas kernels: 59.7 us -> 57.8 us  [the longest x1 56.6 us: body(): pl.pallas_call(step_kernel, out_shape=(jax.ShapeDtypeStruct((tokens, widt...]
where the time goes in v2:
time: 58.8 us; the launch traced here: 58.4 us
  Pallas kernels  57.8 us (98%)
  between operations  0.64 us (1%)
    pallas_call x1, Pallas kernels, body(): pl.pallas_call(step_kernel, out_shape=(jax.ShapeDtypeStruct((tokens, widt...  56.6 us

profile of v2, /device:TPU:1, one launch (start us, length us, event | category | flops | bytes accessed | tf_op | source)
XLA Modules:
  0.0 58.4 jit_solution(8639975546125655262)
XLA Ops:
  0.6 56.6 %distill_step.1 = (bf16[128,768]{1,0:T(8,128)(2,1)S(1)}, bf16[8,16,256]{2,1,0:T(8,128)(2,1)S(1)}, f32[192,768]{1,0:T(8,128)S(1)}, f32[64,768]{1,0:T(8,128)S(1)}) custom-call(bf16[128,768]{1,0:T(8,128)(2,1)} %x_h.1, bf16[64,128]{1,0:T(8,128)(2,1)} %th_h.1, bf16[192,768]{1,0:T(8,128)(2,1)} %wu_h.1, bf16[192,768]{1,0:T(8,128)(2,1)} %wd_h.1, bf16[64,768]{1,0:T(8,128)(2,1)} %wp_h.1), custom_call_target="tpu_custom_call" | custom-call | tf_op jit(solution)/shard_map/distill_step/pallas_call | solution.py:319
  57.3 1.1 %grad_up.1 = (f32[192,768]{1,0:T(8,128)}, f32[192,768]{1,0:T(8,128)}, f32[64,768]{1,0:T(8,128)}) custom-call(bf16[8,16,256]{2,1,0:T(8,128)(2,1)S(1)} %get-tuple-element.7.dpt, bf16[128,768]{1,0:T(8,128)(2,1)S(1)} %get-tuple-element.8.x, f32[192,768]{1,0:T(8,128)S(1)} %get-tuple-element.9.gd, f32[64,768]{1,0:T(8,128)S(1)} %get-tuple-element.10.gp), custom_call_target="tpu_custom_call" | custom-call | tf_op jit(solution)/shard_map/grad_up/pallas_call | solution.py:334

commit v3 on v2

--- a/solution.py
+++ b/solution.py
@@ -37,9 +37,9 @@
     x, dpt, gd, gp,
     th, wu, wd, wp,
     pre_s, pre_r, act, hid, ht, ht2, tgt, tgt_r,
-    res_s, res_r, win, far_r, piece, dfull, dh_s, dh_r,
+    res_s, res_r, win, far_r, piece, dfull, dh_s, dh_f, dh_p, dh_r,
     go, in_sem, core_ss, core_rs,
-    a1_ss, a1_rs, a2_ss, a2_rs, b1_ss, b1_rs, b2_ss, b2_rs, c_ss, c_rs, d1_ss, d1_rs, d2_ss, d2_rs,
+    a1_ss, a1_rs, a2_ss, a2_rs, b1_ss, b1_rs, b2_ss, b2_rs, c_ss, c_rs, d1_ss, d1_rs, act_ss, act_rs,
 ):
     ff = wu.shape[0]
     half = x.shape[0] // 2
@@ -154,7 +154,7 @@
     def _():
         give.start()
 
-    act[...] = 2.0 * active
+    act[mp] = 2.0 * active
 
     @pl.when(c == 1)
     def _():
@@ -198,6 +198,10 @@
     for j, (dz, dy) in enumerate(FAR):
         zz, yy = at(dz, dy)
         sent_b.append(send(win, far_r.at[j], b2_ss.at[j], b2_rs.at[j], device(zz, yy, c, mp)))
+    sent_act = []
+    for d in MP_ORDER:
+        mm = lax.rem(mp + d, NM)
+        sent_act.append(send(act.at[mp], act.at[mp], act_ss.at[d], act_rs.at[mp], device(z, y, c, mm)))
     left(sent_b[: len(WINDOW)])
     residual = total
     for j in range(len(FAR)):
@@ -217,48 +221,26 @@
     def d_half(i, h):
         return dfull[i, groups * h : groups * h + groups].reshape(half, cols)
 
+    def packed(rows):
+        low, high = rows[:, :128], rows[:, 128:]
+        return jnp.concatenate([low, jnp.concatenate([high[: half // 2], high[half // 2 :]], axis=1)], axis=0)
+
     d_own = [d_half(c, h) for h in range(2)]
     sent_d = []
     for e in (1, 0):
         i = lax.rem(c + e, NC)
-        part = nt(d_own[0], wd[i, :, :cols]) + nt(d_own[1], wd[i, :, cols:])
-        dh_s[i, :, :, :ff] = part.reshape(quarter, 16, ff)
-        for d in (2, 1, 3, 0):
-            if e or d:
-                t = lax.rem(tok + d, quarter)
-                dev = device(z, y, i, c * quarter + t)
-                sent_d.append(send(dh_s.at[i, t], dh_r.at[mp], d1_ss.at[e * quarter + d], d1_rs.at[mp], dev))
-    keep2 = pltpu.make_async_copy(dh_s.at[c, tok], dh_r.at[mp], d1_rs.at[mp])
-    give2 = pltpu.make_async_remote_copy(
-        src_ref=dh_s.at[c, tok], dst_ref=dh_r.at[mp], send_sem=d1_ss.at[0], recv_sem=d1_rs.at[mp],
-        device_id=device(z, y, c, c * quarter + tok), device_id_type=MESH,
-    )
-
-    @pl.when(own_half == c)
-    def _():
-        keep2.start()
-
-    @pl.when(own_half != c)
-    def _():
-        give2.start()
-
+        part = packed(nt(d_own[0], wd[i, :, :cols]) + nt(d_own[1], wd[i, :, cols:]))
+        dh_s[e] = part.astype(BF16)
+        dh_f[e] = part
+        for d in MP_ORDER:
+            mm = lax.rem(mp + d, NM)
+            k = e * NM + d
+            sent_d.append(send(dh_s.at[e], dh_r.at[c, mp], d1_ss.at[k], d1_rs.at[c * NM + mp], device(z, y, i, mm)))
+        if e:
+            sent_d.append(send(dh_f.at[e], dh_p, core_ss.at[4], core_rs.at[4], partner))
     sent.append(send(dfull.at[c], dfull.at[c], core_ss.at[3], core_rs.at[3], partner))
     left(sent)
-    total = None
-    for m in range(NM):
-        arrived(dh_r.at[m], d1_rs.at[m])
-        total = dh_r[m] if total is None else total + dh_r[m]
-    dpt[mp] = (total * act[...]).astype(BF16)
-    sent = []
-    for d in MP_ORDER:
-        mm = lax.rem(mp + d, NM)
-        sent.append(send(dpt.at[mp], dpt.at[mp], d2_ss.at[d], d2_rs.at[mp], device(z, y, c, mm)))
-
-    left(sent_d)
-
-    @pl.when(own_half != c)
-    def _():
-        give2.wait_send()
+    left(sent_act)
 
     arrived(dfull.at[oc], core_rs.at[3])
     arrived(ht2, core_rs.at[2])
@@ -268,11 +250,24 @@
         d_nat = [d_half(i, h) for i in range(NC)]
         gd[:, cols * h : cols * h + cols] = tn(h_own, d_half(c, h)) + tn(h_other, d_half(oc, h))
         gp[:, cols * h : cols * h + cols] = -(nn(th[:, :half], d_nat[0]) + nn(th[:, half:], d_nat[1]))
-
-    for d in MP_ORDER:
-        mm = lax.rem(mp + d, NM)
-        arrived(dpt.at[mm], d2_rs.at[mm])
-    left(sent)
+    for d in MP_ORDER:
+        mm = lax.rem(mp + d, NM)
+        arrived(act.at[mm], act_rs.at[mm])
+
+    arrived(dh_p, core_rs.at[4])
+    for e in range(NC):
+        i = lax.rem(c + e, NC)
+        total = dh_f[0] if e == 0 else dh_p[...]
+        for d in reversed(MP_ORDER):
+            mm = lax.rem(mp + d, NM)
+            arrived(dh_r.at[i, mm], d1_rs.at[i * NM + mm])
+            total = total + dh_r[i, mm].astype(F32)
+        gate = act[pl.ds(i * quarter, quarter)].reshape(half, act.shape[-1])
+        high = total[half:]
+        high = jnp.concatenate([high[:, : ff - 128], high[:, ff - 128 :]], axis=0)
+        dpt[i, :, :128] = (total[:half] * gate[:, :128]).astype(BF16)
+        dpt[i, :, 128:ff] = (high * gate[:, 128:ff]).astype(BF16)
+    left(sent_d)
 
 
 def last_kernel(dpt, x, gd, gp, gu_h, gd_h, gp_h, gu, sem):
@@ -297,7 +292,7 @@
     tokens, width = student_in.shape
     ff, td = w_up.shape[0], w_proj.shape[0]
     half, cols = tokens // 2, width // 2
-    wide = 256
+    wide, fold = 256, half * ff // 128
     hbm, vmem = pl.BlockSpec(memory_space=pltpu.HBM), pl.BlockSpec(memory_space=pltpu.VMEM)
     any_ = pl.BlockSpec(memory_space=pl.ANY)
     sem = pltpu.SemaphoreType.DMA
@@ -305,22 +300,22 @@
     scratch = [
         vm((td, tokens), BF16), vm((ff, width), BF16), vm((NC, ff, width), BF16),
         vm((td, width), BF16),
-        vm((NM, 16, wide), F32), vm((NM, 16, wide), F32), vm((16, wide), F32), vm((16, wide), BF16),
+        vm((NM, 16, wide), F32), vm((NM, 16, wide), F32), vm((NM, 16, wide), F32), vm((16, wide), BF16),
         vm((NC, NM // 2, 16, wide), BF16), vm((NM // 2, 16, wide), BF16),
         vm((NC, half, width), F32), vm((half, width), F32),
         vm((16, 8, cols), F32), vm((15, 8, cols), F32), vm((8, cols), F32), vm((3, 8, cols), F32),
         vm((8, cols), BF16), vm((NC, 16, 8, cols), BF16),
-        vm((NC, NM // 2, 16, wide), F32), vm((NM, 16, wide), F32),
-        pltpu.SemaphoreType.REGULAR, sem((5,)), sem((4,)), sem((4,)),
+        vm((NC, fold, 128), BF16), vm((NC, fold, 128), F32), vm((fold, 128), F32), vm((NC, NM, fold, 128), BF16),
+        pltpu.SemaphoreType.REGULAR, sem((5,)), sem((5,)), sem((5,)),
         sem((8,)), sem((8,)), sem((8,)), sem((8,)), sem((15,)), sem((15,)), sem((3,)), sem((3,)),
-        sem((15,)), sem((15,)), sem((8,)), sem((8,)), sem((8,)), sem((8,)),
+        sem((15,)), sem((15,)), sem((16,)), sem((16,)), sem((8,)), sem((8,)),
     ]
     grads = [jax.ShapeDtypeStruct((rows, width), F32) for rows in (ff, ff, td)]
     x, dpt, gd, gp = pl.pallas_call(
         step_kernel,
         out_shape=(
             jax.ShapeDtypeStruct((tokens, width), BF16),
-            jax.ShapeDtypeStruct((NM, 16, wide), BF16),
+            jax.ShapeDtypeStruct((NC, half, wide), BF16),
             *grads[1:],
         ),
         in_specs=[hbm] * 5,

time: 58.8 us -> 57.9 us (0.985)
  Pallas kernels: 57.8 us -> 57.1 us
    pallas_call x1, Pallas kernels: 56.6 us -> 56 us  [body(): pl.pallas_call(step_kernel, out_shape=(jax.ShapeDtypeStruct((tokens, widt...]
where the time goes in v3:
time: 57.9 us; the launch traced here: 57.7 us
  Pallas kernels  57.1 us (99%)
  between operations  0.64 us (1%)
    pallas_call x1, Pallas kernels, body(): pl.pallas_call(step_kernel, out_shape=(jax.ShapeDtypeStruct((tokens, widt...  56 us

profile of v3, /device:TPU:1, one launch (start us, length us, event | category | flops | bytes accessed | tf_op | source)
XLA Modules:
  0.0 57.7 jit_solution(5436625858961224137)
XLA Ops:
  0.6 56.0 %distill_step.1 = (bf16[128,768]{1,0:T(8,128)(2,1)S(1)}, bf16[2,64,256]{2,1,0:T(8,128)(2,1)S(1)}, f32[192,768]{1,0:T(8,128)S(1)}, f32[64,768]{1,0:T(8,128)S(1)}) custom-call(bf16[128,768]{1,0:T(8,128)(2,1)} %x_h.1, bf16[64,128]{1,0:T(8,128)(2,1)} %th_h.1, bf16[192,768]{1,0:T(8,128)(2,1)} %wu_h.1, bf16[192,768]{1,0:T(8,128)(2,1)} %wd_h.1, bf16[64,768]{1,0:T(8,128)(2,1)} %wp_h.1), custom_call_target="tpu_custom_call" | custom-call | tf_op jit(solution)/shard_map/distill_step/pallas_call | solution.py:314
  56.6 1.1 %grad_up.1 = (f32[192,768]{1,0:T(8,128)}, f32[192,768]{1,0:T(8,128)}, f32[64,768]{1,0:T(8,128)}) custom-call(bf16[2,64,256]{2,1,0:T(8,128)(2,1)S(1)} %get-tuple-element.7.dpt, bf16[128,768]{1,0:T(8,128)(2,1)S(1)} %get-tuple-element.8.x, f32[192,768]{1,0:T(8,128)S(1)} %get-tuple-element.9.gd, f32[64,768]{1,0:T(8,128)S(1)} %get-tuple-element.10.gp), custom_call_target="tpu_custom_call" | custom-call | tf_op jit(solution)/shard_map/grad_up/pallas_call | solution.py:329

commit v4 on v3

--- a/solution.py
+++ b/solution.py
@@ -227,17 +227,15 @@
 
     d_own = [d_half(c, h) for h in range(2)]
     sent_d = []
-    for e in (1, 0):
-        i = lax.rem(c + e, NC)
+    for i in (1, 0):
         part = packed(nt(d_own[0], wd[i, :, :cols]) + nt(d_own[1], wd[i, :, cols:]))
-        dh_s[e] = part.astype(BF16)
-        dh_f[e] = part
-        for d in MP_ORDER:
-            mm = lax.rem(mp + d, NM)
-            k = e * NM + d
-            sent_d.append(send(dh_s.at[e], dh_r.at[c, mp], d1_ss.at[k], d1_rs.at[c * NM + mp], device(z, y, i, mm)))
-        if e:
-            sent_d.append(send(dh_f.at[e], dh_p, core_ss.at[4], core_rs.at[4], partner))
+        dh_s[i] = part.astype(BF16)
+        dh_f[i] = part
+        for k in range(NM - 1):
+            mm = k + jnp.where(k >= mp, 1, 0)
+            ss = d1_ss.at[i * NM + k]
+            sent_d.append(send(dh_s.at[i], dh_r.at[c, mp], ss, d1_rs.at[c * NM + mp], device(z, y, i, mm)))
+    sent_d.append(send(dh_f.at[oc], dh_p, core_ss.at[4], core_rs.at[4], partner))
     sent.append(send(dfull.at[c], dfull.at[c], core_ss.at[3], core_rs.at[3], partner))
     left(sent)
     left(sent_act)
@@ -257,9 +255,9 @@
     arrived(dh_p, core_rs.at[4])
     for e in range(NC):
         i = lax.rem(c + e, NC)
-        total = dh_f[0] if e == 0 else dh_p[...]
-        for d in reversed(MP_ORDER):
-            mm = lax.rem(mp + d, NM)
+        total = dh_f[c] if e == 0 else dh_p[...]
+        for k in range(NM - 1):
+            mm = k + jnp.where(k >= mp, 1, 0)
             arrived(dh_r.at[i, mm], d1_rs.at[i * NM + mm])
             total = total + dh_r[i, mm].astype(F32)
         gate = act[pl.ds(i * quarter, quarter)].reshape(half, act.shape[-1])

time: 57.9 us -> 57 us (0.984)
  Pallas kernels: 57.1 us -> 56.2 us
    pallas_call x1, Pallas kernels: 56 us -> 55 us  [body(): pl.pallas_call(step_kernel, out_shape=(jax.ShapeDtypeStruct((tokens, widt...]
where the time goes in v4:
time: 57 us; the launch traced here: 56.8 us
  Pallas kernels  56.2 us (99%)
  between operations  0.64 us (1%)
    pallas_call x1, Pallas kernels, body(): pl.pallas_call(step_kernel, out_shape=(jax.ShapeDtypeStruct((tokens, widt...  55 us

profile of v4, /device:TPU:1, one launch (start us, length us, event | category | flops | bytes accessed | tf_op | source)
XLA Modules:
  0.0 56.8 jit_solution(6951480076344485976)
XLA Ops:
  0.6 55.0 %distill_step.1 = (bf16[128,768]{1,0:T(8,128)(2,1)S(1)}, bf16[2,64,256]{2,1,0:T(8,128)(2,1)S(1)}, f32[192,768]{1,0:T(8,128)S(1)}, f32[64,768]{1,0:T(8,128)S(1)}) custom-call(bf16[128,768]{1,0:T(8,128)(2,1)} %x_h.1, bf16[64,128]{1,0:T(8,128)(2,1)} %th_h.1, bf16[192,768]{1,0:T(8,128)(2,1)} %wu_h.1, bf16[192,768]{1,0:T(8,128)(2,1)} %wd_h.1, bf16[64,768]{1,0:T(8,128)(2,1)} %wp_h.1), custom_call_target="tpu_custom_call" | custom-call | tf_op jit(solution)/shard_map/distill_step/pallas_call | solution.py:312
  55.7 1.1 %grad_up.1 = (f32[192,768]{1,0:T(8,128)}, f32[192,768]{1,0:T(8,128)}, f32[64,768]{1,0:T(8,128)}) custom-call(bf16[2,64,256]{2,1,0:T(8,128)(2,1)S(1)} %get-tuple-element.7.dpt, bf16[128,768]{1,0:T(8,128)(2,1)S(1)} %get-tuple-element.8.x, f32[192,768]{1,0:T(8,128)S(1)} %get-tuple-element.9.gd, f32[64,768]{1,0:T(8,128)S(1)} %get-tuple-element.10.gp), custom_call_target="tpu_custom_call" | custom-call | tf_op jit(solution)/shard_map/grad_up/pallas_call | solution.py:327

commit v5 on v4

--- a/solution.py
+++ b/solution.py
@@ -48,7 +48,7 @@
     dp, mp = lax.axis_index("dp"), lax.axis_index("mp")
     z, y, c = dp // (NY * NC), (dp // NC) % NY, dp % NC
     oc = 1 - c
-    mirror = 1 - 2 * c
+    turn = 1 - 2 * (lax.rem(z, 4) // 2)
     own_half = mp // quarter
     tok = mp % quarter
 
@@ -60,7 +60,8 @@
     loads[1].start()
 
     def at(dz, dy, sign=1):
-        return lax.rem(z + sign * mirror * dz + NZ, NZ), lax.rem(y + sign * dy + NY, NY)
+        step = turn * dz if dz == 2 and dy else sign * dz
+        return lax.rem(z + step + NZ, NZ), lax.rem(y + sign * dy + NY, NY)
 
     def device(zz, yy, cc, mm):
         return (zz * (NY * NC) + yy * NC + cc, mm)

time: 57 us -> 56.8 us (level)
  no operation moved by 1% of the time
where the time goes in v5:
time: 56.8 us; the launch traced here: 56.5 us
  Pallas kernels  55.8 us (98%)
  between operations  0.64 us (1%)
    pallas_call x1, Pallas kernels, body(): pl.pallas_call(step_kernel, out_shape=(jax.ShapeDtypeStruct((tokens, widt...  54.7 us

profile of v5, /device:TPU:1, one launch (start us, length us, event | category | flops | bytes accessed | tf_op | source)
XLA Modules:
  0.0 56.5 jit_solution(2007970499996321706)
XLA Ops:
  0.6 54.7 %distill_step.1 = (bf16[128,768]{1,0:T(8,128)(2,1)S(1)}, bf16[2,64,256]{2,1,0:T(8,128)(2,1)S(1)}, f32[192,768]{1,0:T(8,128)S(1)}, f32[64,768]{1,0:T(8,128)S(1)}) custom-call(bf16[128,768]{1,0:T(8,128)(2,1)} %x_h.1, bf16[64,128]{1,0:T(8,128)(2,1)} %th_h.1, bf16[192,768]{1,0:T(8,128)(2,1)} %wu_h.1, bf16[192,768]{1,0:T(8,128)(2,1)} %wd_h.1, bf16[64,768]{1,0:T(8,128)(2,1)} %wp_h.1), custom_call_target="tpu_custom_call" | custom-call | tf_op jit(solution)/shard_map/distill_step/pallas_call | solution.py:313
  55.3 1.1 %grad_up.1 = (f32[192,768]{1,0:T(8,128)}, f32[192,768]{1,0:T(8,128)}, f32[64,768]{1,0:T(8,128)}) custom-call(bf16[2,64,256]{2,1,0:T(8,128)(2,1)S(1)} %get-tuple-element.7.dpt, bf16[128,768]{1,0:T(8,128)(2,1)S(1)} %get-tuple-element.8.x, f32[192,768]{1,0:T(8,128)S(1)} %get-tuple-element.9.gd, f32[64,768]{1,0:T(8,128)S(1)} %get-tuple-element.10.gp), custom_call_target="tpu_custom_call" | custom-call | tf_op jit(solution)/shard_map/grad_up/pallas_call | solution.py:328

commit v6 on v5

--- a/solution.py
+++ b/solution.py
@@ -13,7 +13,7 @@
 MESH = pl.DeviceIdType.MESH
 
 WINDOW = (
-    (0, 2), (2, 1), (2, -1), (3, 0), (-3, 0), (1, 1), (1, -1), (-1, 1), (-1, -1),
+    (1, 1), (1, -1), (-1, 1), (-1, -1), (0, 2), (2, 1), (2, -1), (3, 0), (-3, 0),
     (2, 0), (-2, 0), (0, 1), (0, -1), (1, 0), (-1, 0),
 )
 FAR = ((8, 0), (4, 2), (-4, 2))

time: 56.8 us -> 56.6 us (level)
  no operation moved by 1% of the time
where the time goes in v6:
time: 56.6 us; the launch traced here: 56.5 us
  Pallas kernels  55.8 us (99%)
  between operations  0.64 us (1%)
    pallas_call x1, Pallas kernels, body(): pl.pallas_call(step_kernel, out_shape=(jax.ShapeDtypeStruct((tokens, widt...  54.7 us

profile of v6, /device:TPU:1, one launch (start us, length us, event | category | flops | bytes accessed | tf_op | source)
XLA Modules:
  0.0 56.5 jit_solution(15820262568191763180)
XLA Ops:
  0.6 54.7 %distill_step.1 = (bf16[128,768]{1,0:T(8,128)(2,1)S(1)}, bf16[2,64,256]{2,1,0:T(8,128)(2,1)S(1)}, f32[192,768]{1,0:T(8,128)S(1)}, f32[64,768]{1,0:T(8,128)S(1)}) custom-call(bf16[128,768]{1,0:T(8,128)(2,1)} %x_h.1, bf16[64,128]{1,0:T(8,128)(2,1)} %th_h.1, bf16[192,768]{1,0:T(8,128)(2,1)} %wu_h.1, bf16[192,768]{1,0:T(8,128)(2,1)} %wd_h.1, bf16[64,768]{1,0:T(8,128)(2,1)} %wp_h.1), custom_call_target="tpu_custom_call" | custom-call | tf_op jit(solution)/shard_map/distill_step/pallas_call | solution.py:313
  55.4 1.1 %grad_up.1 = (f32[192,768]{1,0:T(8,128)}, f32[192,768]{1,0:T(8,128)}, f32[64,768]{1,0:T(8,128)}) custom-call(bf16[2,64,256]{2,1,0:T(8,128)(2,1)S(1)} %get-tuple-element.7.dpt, bf16[128,768]{1,0:T(8,128)(2,1)S(1)} %get-tuple-element.8.x, f32[192,768]{1,0:T(8,128)S(1)} %get-tuple-element.9.gd, f32[64,768]{1,0:T(8,128)S(1)} %get-tuple-element.10.gp), custom_call_target="tpu_custom_call" | custom-call | tf_op jit(solution)/shard_map/grad_up/pallas_call | solution.py:328
